TPU v7x, 256 devices: a whole 4x4x8 slice. The times are simulated.
256 devices in a mesh: patch: 32 (over y, z), batch: 8 (over x, core).
Axes of the slice: x: 4, y: 4, z: 8, core: 2. Of those that a mesh axis runs over, the one named last changes fastest.
Arguments:
- hidden_in: bfloat16 [32768, 1536], P(('batch', 'patch')), parts along dimension 0, may hold values from -6 to 6
- queries: bfloat16 [32768, 768], P(('batch', 'patch')), parts along dimension 0, may hold values from -40 to 40
- fresh_kv: bfloat16 [32768, 1536], P(('batch', 'patch')), parts along dimension 0, may hold values from -144 to 144
- stale_kv: bfloat16 [32768, 1536], P(('batch', 'patch')), parts along dimension 0, may hold values from -144 to 144
- modulation: float32 [16, 1536], P('batch'), parts along dimension 0, may hold values from -3 to 3
- w_out: bfloat16 [768, 1536], replicated, may hold values from -0.21875 to 0.21875
- router: float32 [1536, 16], replicated, may hold values from -0.15625 to 0.15625
- fc_in: bfloat16 [32, 1536, 1536], P('patch'), may hold values from -0.15625 to 0.15625
- fc_out: bfloat16 [32, 1536, 1536], P('patch'), may hold values from -0.109375 to 0.109375
- expert_ids: int32 [32768, 2], P(('batch', 'patch')), parts along dimension 0, may hold values from 0 to 15, all different within a row; in each aligned block of 128 rows (0 to 127, 128 to 255, ...) at most 32 rows name the same one
Outputs:
- attended: bfloat16 [32768, 768], P(('batch', 'patch')), parts along dimension 0
- mixed: bfloat16 [32768, 1536], P(('batch', 'patch')), parts along dimension 0
There are 8 independent parts, one for each index of `batch`. A program takes and returns all parts, laid end to end along the dimension named above; an argument that names none is the same for every part. Nothing has to cross between parts.
Inputs may be any that keep to these rules, and one draw needn't show every extreme that they name: `expert_ids`: within each aligned block of 128 rows (the rows of one index of patch) no expert is named more than 32 times; the two experts of a row differ.
All inputs are finite; a program needn't handle non-finite values.
Results may differ from a plain program's by a relative error of at most 0.007.
Values may be sent and summed in bfloat16 or wider, within the bound.
No kernel may reach another device: no remote copies, remote signals or barrier semaphores. Data moves between devices by JAX's collectives and lax.ppermute only.
A program may use at most 128 MiB of HBM per device.

v0:
```python
import jax
import jax.numpy as jnp
from jax import lax
from jax.sharding import PartitionSpec as P

HEADS = 8


def attend_block(query_rows, view):
    count = query_rows.shape[0]
    width = query_rows.shape[1]
    head_size = width // HEADS
    qh = query_rows.reshape(count, HEADS, head_size)
    kh = view[:, :width].reshape(-1, HEADS, head_size)
    vh = view[:, width:].reshape(-1, HEADS, head_size)
    scores = jnp.einsum("qhd,khd->hqk", qh, kh, preferred_element_type=jnp.float32) * (
        1.0 / head_size**0.5
    )
    weights = jax.nn.softmax(scores, axis=-1).astype(jnp.bfloat16)
    out = jnp.einsum("hqk,khd->qhd", weights, vh, preferred_element_type=jnp.float32)
    return out.reshape(count, width).astype(jnp.bfloat16)


def per_device(
    hidden_in, queries, fresh_kv, stale_kv, modulation, w_out, router, fc_in, fc_out, expert_ids
):
    rows = queries.shape[0]
    width = hidden_in.shape[1]
    experts = router.shape[1]
    capacity = 4 * rows // experts
    patch_index = lax.axis_index("patch")
    gathered = lax.all_gather(stale_kv, "patch", axis=0, tiled=True)
    view = lax.dynamic_update_slice_in_dim(gathered, fresh_kv, patch_index * rows, 0)
    attended = attend_block(queries, view)
    resid = hidden_in.astype(jnp.float32) + jnp.dot(
        attended, w_out, preferred_element_type=jnp.float32
    )
    mean = jnp.mean(resid, axis=-1, keepdims=True)
    centered = resid - mean
    var = jnp.mean(centered * centered, axis=-1, keepdims=True)
    normed = (centered * lax.rsqrt(var + 1e-06) * (1.0 + modulation[0]) + modulation[1]).astype(
        jnp.bfloat16
    )
    logits = jnp.dot(normed.astype(jnp.float32), router, precision=lax.Precision.HIGHEST)
    chosen = jnp.take_along_axis(logits, expert_ids, axis=1)
    first_gate = jax.nn.sigmoid(chosen[:, 0] - chosen[:, 1])
    gates = jnp.stack([first_gate, 1.0 - first_gate], axis=1)
    onehot = (expert_ids.reshape(-1, 1) == jnp.arange(experts, dtype=jnp.int32)[None, :]).astype(
        jnp.int32
    )
    before = jnp.cumsum(onehot, axis=0) - onehot
    slots = jnp.sum(before * onehot, axis=1)
    position = expert_ids.reshape(-1) * capacity + slots
    buffer = (
        jnp.zeros((experts * capacity, width), jnp.bfloat16)
        .at[position]
        .set(jnp.repeat(normed, 2, axis=0))
    )
    outgoing = jnp.broadcast_to(
        buffer.reshape(experts, 1, capacity, width), (experts, 2, capacity, width)
    )
    outgoing = outgoing.reshape(2 * experts, capacity, width)
    block = lax.all_to_all(outgoing, "patch", split_axis=0, concat_axis=0, tiled=True)
    flat = block.reshape(-1, width)
    hidden = jax.nn.gelu(
        jnp.dot(flat, fc_in[0], preferred_element_type=jnp.float32), approximate=True
    ).astype(jnp.bfloat16)
    back = lax.all_to_all(
        jnp.dot(hidden, fc_out[0], preferred_element_type=jnp.float32)
        .reshape(block.shape[:-1] + (width,))
        .astype(jnp.bfloat16),
        "patch",
        split_axis=0,
        concat_axis=0,
        tiled=True,
    ).astype(jnp.float32)
    totals = jnp.sum(back.reshape(experts, 2, capacity, width), axis=1).reshape(
        experts * capacity, width
    )
    picked = jnp.take(totals, position, axis=0).reshape(rows, 2, width)
    moe = jnp.sum(gates[:, :, None] * picked, axis=1)
    mixed = (resid + moe).astype(jnp.bfloat16)
    return (attended, mixed)


def solution(mesh):
    return jax.shard_map(
        per_device,
        mesh=mesh,
        in_specs=(
            P(("batch", "patch"), None),
            P(("batch", "patch"), None),
            P(("batch", "patch"), None),
            P(("batch", "patch"), None),
            P("batch", None),
            P(),
            P(),
            P("patch", None, None),
            P("patch", None, None),
            P(("batch", "patch"), None),
        ),
        out_specs=(P(("batch", "patch"), None), P(("batch", "patch"), None)),
        check_vma=False,
    )
```

profile of v0, /device:TPU:2, one launch (start us, length us, event | category | flops | bytes accessed | tf_op | source)
XLA Modules:
  0.0 388.5 jit_solution(3229449977234668653)
XLA Ops:
  7.2 0.7 all-gather.2.cloned.1.call-update
  7.9 0.8 copy.71
  9.0 1.1 copy.66
  10.1 0.7 broadcast_multiply_fusion
  11.0 0.6 reduce-window.6
  11.9 0.8 add_reduce_fusion
  12.8 120.5 %all-gather.2.cloned.1.call-done = bf16[4096,1536]{1,0:T(8,128)(2,1)} async-done(((bf16[128,1536]{1,0:T(8,128)(2,1)}), bf16[4096,1536]{1,0:T(8,128)(2,1)}) %all-gather.2.cloned.1.call-update) | async-done | bytes 12582928 | tf_op jit(solution)/shard_map/all_gather | solution.py:32
  133.3 1.8 constant_dynamic-update-slice_fusion
  135.1 10.3 %fusion.35 = (bf16[4096,768]{1,0:T(8,128)(2,1)}, bf16[4096,768]{1,0:T(8,128)(2,1)}) fusion(bf16[4096,1536]{1,0:T(8,128)(2,1)} %constant_dynamic-update-slice_fusion), kind=kLoop, calls=%fused_computation.62 | loop fusion | bytes 25165824 | tf_op jit(solution)/shard_map/slice | solution.py:14
  145.4 8.8 %copy.64 = bf16[4096,768]{0,1:T(8,128)(2,1)} copy(bf16[4096,768]{1,0:T(8,128)(2,1)} %get-tuple-element.17) | data formatting | bytes 12582912 | tf_op jit(solution)/shard_map/slice | solution.py:15
  154.1 8.6 %copy.65 = bf16[4096,768]{0,1:T(8,128)(2,1)} copy(bf16[4096,768]{1,0:T(8,128)(2,1)} %get-tuple-element.16) | data formatting | bytes 12582912 | tf_op jit(solution)/shard_map/slice | solution.py:14
  162.8 11.5 %fusion.36 = (f32[8,128]{1,0:T(8,128)S(1)}, f32[8,128,4096]{1,2,0:T(8,128)}) fusion(bf16[4096,8,96]{0,2,1:T(8,128)(2,1)} %bitcast.75, bf16[128,8,96]{0,2,1:T(8,128)(2,1)S(1)} %bitcast.80), kind=kOutput, calls=%fused_computation.63 | convolution fusion | flops 817893376 | bytes 23269376 | tf_op jit(solution)/shard_map/sub | solution.py:19
  174.3 10.2 %fusion.27 = bf16[8,96,128]{2,1,0:T(8,128)(2,1)S(1)} fusion(bf16[4096,8,96]{0,2,1:T(8,128)(2,1)} %bitcast.74, f32[8,128,4096]{1,2,0:T(8,128)} %get-tuple-element.19, f32[8,128]{1,0:T(8,128)S(1)} %get-tuple-element.18), kind=kOutput, calls=%fused_computation.30 | convolution fusion | flops 813793280 | bytes 23269376 | tf_op jit(solution)/shard_map/hqk,khd->qhd/dot_general | solution.py:20
  184.6 0.6 fusion.37
  185.2 0.2 multiply_reduce_fusion.1
  185.6 0.4 broadcast_in_dim.38
  186.0 1.2 reshape.156
  187.2 2.9 scatter_custom_fusion
  190.1 0.4 broadcast_in_dim.40
  190.5 78.9 %all_to_all.10 = bf16[32,32,1536]{2,1,0:T(8,128)(2,1)S(1)} all-to-all(bf16[32,32,1536]{2,1,0:T(8,128)(2,1)S(1)} %bitcast.73), channel_id=1, replica_groups=mesh['patch'=32,'batch'=8] {'patch'}, dimensions={0} | all-to-all | bytes 6291456 | tf_op jit(solution)/shard_map/all_to_all | solution.py:63
  269.4 8.7 %fusion.15 = bf16[1024,1536]{1,0:T(8,128)(2,1)S(1)} fusion(bf16[1024,1536]{1,0:T(8,128)(2,1)S(1)} %bitcast.77, bf16[1,1536,1536]{2,1,0:T(8,128)(2,1)} %param.17), kind=kOutput, calls=%fused_computation.20 | convolution fusion | flops 4845993984 | bytes 11010048 | tf_op jit(solution)/shard_map/dot_general | solution.py:66
  278.2 6.4 %fusion.22 = bf16[32,32,1536]{2,1,0:T(8,128)(2,1)} fusion(bf16[32,32,1536]{2,1,0:T(8,128)(2,1)S(1)} %bitcast.86, bf16[1,1536,1536]{2,1,0:T(8,128)(2,1)S(1)} %bitcast.85), kind=kOutput, calls=%fused_computation.26 | convolution fusion | flops 4833411072 | bytes 11010048 | tf_op jit(solution)/shard_map/dot_general | solution.py:69
  284.6 5.2 %all-to-all-start.1 = ((bf16[32,32,1536]{2,1,0:T(8,128)(2,1)}), bf16[32,32,1536]{2,1,0:T(8,128)(2,1)}, u32[]{:S(2)}, u32[]{:S(2)}) async-start(bf16[32,32,1536]{2,1,0:T(8,128)(2,1)} %fusion.22), calls=%async_computation.1 | async-start | bytes 6291456 | tf_op jit(solution)/shard_map/all_to_all | solution.py:68
  290.4 0.8 copy.77
  291.3 0.4 fusion.38
  291.7 2.0 gather_fusion.1
  294.1 69.8 %all-to-all-done.1 = bf16[32,32,1536]{2,1,0:T(8,128)(2,1)} async-done(((bf16[32,32,1536]{2,1,0:T(8,128)(2,1)}), bf16[32,32,1536]{2,1,0:T(8,128)(2,1)}, u32[]{:S(2)}, u32[]{:S(2)}) %all-to-all-start.1) | async-done | bytes 3145760 | tf_op jit(solution)/shard_map/all_to_all | solution.py:68
  363.9 4.5 %convert_reduce_fusion = f32[16,32,1536]{2,1,0:T(8,128)} fusion(bf16[32,32,1536]{2,1,0:T(8,128)(2,1)} %all-to-all-done.1), kind=kLoop, calls=%fused_computation.21 | loop fusion | flops 2359296 | bytes 6291456 | tf_op jit(solution)/shard_map/reduce_sum | solution.py:77
  368.4 5.1 %gather_fusion = f32[256,1536]{1,0:T(8,128)} fusion(f32[512,1536]{1,0:T(8,128)} %bitcast.72, s32[1024]{0:T(1024)S(1)} %pad_clamp_fusion), kind=kCustom, calls=%fused_computation | custom fusion | bytes 3146752 | tf_op jit(solution)/shard_map/jit(_take)/gather | solution.py:80
  373.5 3.0 gather.12
  376.5 4.2 %multiply_reduce_fusion = f32[128,1536]{1,0:T(8,128)S(1)} fusion(f32[128,2,1536]{2,1,0:T(2,128)} %gather.12, pred[128,2]{1,0:T(8,128)(4,1)S(1)} %copy.75, f32[128,2]{1,0:T(8,128)S(1)} %copy.70), kind=kLoop, calls=%fused_computation.28 | loop fusion | flops 983040 | bytes 2360576 | tf_op jit(solution)/shard_map/reduce_sum | solution.py:81
  380.8 0.9 add_convert_fusion
  (43 shorter events, 2.1 us)
Async XLA Ops:
  7.2 177.4 %copy-start = (bf16[768,1536]{1,0:T(8,128)(2,1)S(1)}, bf16[768,1536]{1,0:T(8,128)(2,1)}, u32[]{:S(2)}) copy-start(bf16[768,1536]{1,0:T(8,128)(2,1)} %param.15) | copy-start | bytes 7077892
  7.2 126.1 %all-gather.2.cloned.1.call-start = ((), (), s32[]{:S(2)}) async-start(), calls=%async_computation.2 | async-start | bytes 12976128 | tf_op jit(solution)/shard_map/all_gather | solution.py:32
  174.3 10.2 %copy-start.2 = (bf16[128,1536]{1,0:T(8,128)(2,1)S(1)}, bf16[128,1536]{1,0:T(8,128)(2,1)}, u32[]{:S(2)}) copy-start(bf16[128,1536]{1,0:T(8,128)(2,1)} %param.10) | copy-start | bytes 1179652
  190.5 87.6 %slice-start = ((s8[4718592]{0:T(1024)(128)(4,1)}), s8[524288]{0:T(1024)(128)(4,1)S(1)}, s32[]{:S(2)}) async-start(s8[4718592]{0:T(1024)(128)(4,1)} %bitcast.84), calls=%async_computation.3 | async-start | bytes 1048576
  269.4 8.7 %slice-start.1 = ((s8[4718592]{0:T(1024)(128)(4,1)}), s8[4194304]{0:T(1024)(128)(4,1)S(1)}, s32[]{:S(2)}) async-start(s8[4718592]{0:T(1024)(128)(4,1)} %bitcast.84), calls=%async_computation.4 | async-start | bytes 8388608
  284.6 5.4 %copy-start.4 = (s32[128,2]{0,1:T(2,128)S(1)}, s32[128,2]{0,1:T(2,128)}, u32[]{:S(2)}) copy-start(s32[128,2]{0,1:T(2,128)} %param.19) | copy-start | bytes 3076
  284.6 6.7 %copy-start.3 = (f32[1536,16]{0,1:T(8,128)S(1)}, f32[1536,16]{0,1:T(8,128)}, u32[]{:S(2)}) copy-start(f32[1536,16]{0,1:T(8,128)} %param.16) | copy-start | bytes 294916
  284.6 79.3 %all-to-all-start.1 = ((bf16[32,32,1536]{2,1,0:T(8,128)(2,1)}), bf16[32,32,1536]{2,1,0:T(8,128)(2,1)}, u32[]{:S(2)}, u32[]{:S(2)}) async-start(bf16[32,32,1536]{2,1,0:T(8,128)(2,1)} %fusion.22), calls=%async_computation.1 | async-start | bytes 6291456 | tf_op jit(solution)/shard_map/all_to_all | solution.py:68
  368.4 13.2 %copy-start.1 = (bf16[768,1536]{1,0:T(8,128)(2,1)S(1)}, bf16[768,1536]{1,0:T(8,128)(2,1)}, u32[]{:S(2)}) copy-start(bf16[768,1536]{1,0:T(8,128)(2,1)} %param.15) | copy-start | bytes 7077892
Sparse Core Ops, SparseCore 0:
  10.6 122.6 all-gather.1
where the time goes:
time: 389 us; the launch traced here: 388 us
  waiting for transfers between devices  191 us (49%)
  blocking collectives  78.9 us (20%)
  local copies, waits for them, and re-layouts  48.8 us (13%)
  matrix products  37.9 us (10%)
  between operations  14.3 us (4%)
  other arithmetic  12.3 us (3%)
  starting transfers between devices  5.2 us (1%)
    all_gather x1, waiting for transfers between devices, per_device(): gathered = lax.all_gather(stale_kv, 'patch', axis=0, tiled=True)  121 us
    all_to_all x1, blocking collectives, per_device(): lax.all_to_all(outgoing, 'patch', split_axis=0, concat_axis=0, tiled=True)  78.9 us
    all_to_all x1, waiting for transfers between devices, per_device(): lax.all_to_all(jnp.dot(hidden, fc_out[0], preferred_element_type=jnp.floa...  69.8 us
    slice x2, local copies, waits for them, and re-layouts, attend_block(): kh = view[:, :width].reshape(-1, HEADS, head_size)  18.9 us
    sub x1, matrix products, attend_block(): weights = jax.nn.softmax(scores, axis=-1).astype(jnp.bfloat16)  11.5 us
    dot_general x1, matrix products, attend_block(): jnp.einsum('hqk,khd->qhd', weights, vh, preferred_element_type=jnp.float32)  10.2 us
    slice x1, local copies, waits for them, and re-layouts, attend_block(): vh = view[:, width:].reshape(-1, HEADS, head_size)  8.75 us
    dot_general x1, matrix products, per_device(): jnp.dot(flat, fc_in[0], preferred_element_type=jnp.float32)  8.71 us
  transfers between devices with their start and end apart: 2, of which 2 were waited for; matrix products, arithmetic and copies ran while one was open for 2% of the time, Pallas kernels for 0%

commit v1 on v0

v1 whole, which is shorter than its diff:
```python
import functools

import jax
import jax.numpy as jnp
from jax import lax
from jax.experimental import pallas as pl
from jax.experimental.pallas import tpu as pltpu
from jax.sharding import Mesh, PartitionSpec as P

NY, NZ = 4, 8
HEADS, HEAD = 8, 96
HD = HEADS * HEAD
TOK = 128
D = 1536
ROW = NZ * TOK
EXPERTS, CAP = 16, 32
F32, BF16 = jnp.float32, jnp.bfloat16
EXP2_SCALE = 1.4426950408889634 / HEAD**0.5
VMEM = pl.BlockSpec(memory_space=pltpu.VMEM)
NT = (((1,), (1,)), ((), ()))


def params(*semantics):
    return pltpu.CompilerParams(
        dimension_semantics=semantics or None, vmem_limit_bytes=48 * 1024 * 1024
    )


def split_heads_kernel(*refs):
    ins, out_ref = refs[:-1], refs[-1]
    at = 0
    for ref in ins:
        turned = ref[...].astype(F32).T.astype(BF16)
        for part in range(turned.shape[0] // HD):
            for h in range(HEADS):
                out_ref[h, at : at + HEAD, :] = turned[part * HD + h * HEAD : part * HD + (h + 1) * HEAD]
            at += HEAD


def split_heads(*arrays):
    rows = sum(a.shape[1] for a in arrays) // HEADS
    return pl.pallas_call(
        split_heads_kernel,
        out_shape=jax.ShapeDtypeStruct((HEADS, rows, TOK), BF16),
        in_specs=[VMEM] * len(arrays),
        out_specs=VMEM,
        compiler_params=params(),
    )(*arrays)


def own_row_kernel(qf_ref, kv_ref, q_ref, m_ref, l_ref, acc_ref, kt, vt):
    i = pl.program_id(0)

    @pl.when(i == 0)
    def _():
        for j in range(NZ):
            kt[:, j * TOK : (j + 1) * TOK] = kv_ref[j, :HEAD]
            vt[:, j * TOK : (j + 1) * TOK] = kv_ref[j, HEAD:]

    cols = pl.ds(pl.multiple_of(i * TOK, TOK), TOK)
    kt[:, cols] = qf_ref[0, HEAD : 2 * HEAD]
    vt[:, cols] = qf_ref[0, 2 * HEAD :]
    q = qf_ref[0, :HEAD].astype(F32).T.astype(BF16)
    s = jnp.dot(q, kt[...], preferred_element_type=F32)
    m = jnp.max(s, axis=1, keepdims=True)
    p = jnp.exp2((s - m) * EXP2_SCALE)
    q_ref[...] = q
    m_ref[...] = m
    l_ref[...] = jnp.sum(p, axis=1, keepdims=True)
    acc_ref[...] = lax.dot_general(p.astype(BF16), vt[...], NT, preferred_element_type=F32)
    kt[:, cols] = kv_ref[i, :HEAD]
    vt[:, cols] = kv_ref[i, HEAD:]


def attend_own_row(qf, kv):
    row = lambda width: pl.BlockSpec((TOK, width), lambda i: (i, 0))
    return pl.pallas_call(
        own_row_kernel,
        grid=(NZ,),
        out_shape=(
            jax.ShapeDtypeStruct((ROW, HEAD), BF16),
            jax.ShapeDtypeStruct((ROW, 1), F32),
            jax.ShapeDtypeStruct((ROW, 1), F32),
            jax.ShapeDtypeStruct((ROW, HEAD), F32),
        ),
        in_specs=[
            pl.BlockSpec((1, 3 * HEAD, TOK), lambda i: (i, 0, 0)),
            pl.BlockSpec((NZ, 2 * HEAD, TOK), lambda i: (0, 0, 0)),
        ],
        out_specs=(row(HEAD), row(1), row(1), row(HEAD)),
        scratch_shapes=[pltpu.VMEM((HEAD, ROW), BF16), pltpu.VMEM((HEAD, ROW), BF16)],
        compiler_params=params("arbitrary"),
        cost_estimate=pl.CostEstimate(
            flops=4 * ROW * ROW * HEAD, bytes_accessed=4 << 20, transcendentals=ROW * ROW
        ),
    )(qf, kv)


def other_rows_kernel(last, tile, n, *refs):
    kv_refs = refs[:n]
    q_ref, m_in, l_in, acc_in = refs[n : n + 4]
    outs, (kt, vt) = refs[n + 4 : -2], refs[-2:]

    @pl.when(pl.program_id(0) == 0)
    def _():
        for c, ref in enumerate(kv_refs):
            for j in range(ref.shape[0]):
                at = c * ROW + j * TOK
                kt[:, at : at + TOK] = ref[j, :HEAD]
                vt[:, at : at + TOK] = ref[j, HEAD:]

    q = q_ref[...]
    m, l, acc = m_in[...], l_in[...], acc_in[...]
    for c in range(n):
        cols = slice(c * ROW, (c + 1) * ROW)
        s = jnp.dot(q, kt[:, cols], preferred_element_type=F32)
        top = jnp.maximum(m, jnp.max(s, axis=1, keepdims=True))
        p = jnp.exp2((s - top) * EXP2_SCALE)
        fade = jnp.exp2((m - top) * EXP2_SCALE)
        l = l * fade + jnp.sum(p, axis=1, keepdims=True)
        acc = acc * fade + lax.dot_general(
            p.astype(BF16), vt[:, cols], NT, preferred_element_type=F32
        )
        m = top
    if last:
        outs[0][...] = (acc / l).T.astype(BF16)
    else:
        outs[0][...] = m
        outs[1][...] = l
        outs[2][...] = acc


def attend_other_rows(kvs, state, last, tile=512):
    q, m, l, acc = state
    n = len(kvs)
    row = lambda width: pl.BlockSpec((tile, width), lambda i: (i, 0))
    if last:
        out_shape = (jax.ShapeDtypeStruct((HEAD, ROW), BF16),)
        out_specs = (pl.BlockSpec((HEAD, tile), lambda i: (0, i)),)
    else:
        out_shape = tuple(jax.ShapeDtypeStruct((ROW, w), F32) for w in (1, 1, HEAD))
        out_specs = (row(1), row(1), row(HEAD))
    return pl.pallas_call(
        functools.partial(other_rows_kernel, last, tile, n),
        grid=(ROW // tile,),
        out_shape=out_shape,
        in_specs=[pl.BlockSpec(a.shape, lambda i: (0, 0, 0)) for a in kvs]
        + [row(HEAD), row(1), row(1), row(HEAD)],
        out_specs=out_specs,
        scratch_shapes=[pltpu.VMEM((HEAD, n * ROW), BF16), pltpu.VMEM((HEAD, n * ROW), BF16)],
        compiler_params=params("arbitrary"),
        cost_estimate=pl.CostEstimate(
            flops=4 * ROW * n * ROW * HEAD, bytes_accessed=5 << 20, transcendentals=n * ROW * ROW
        ),
    )(*kvs, q, m, l, acc)


def norm_kernel(pos, hid_ref, att_ref, wo_ref, mod_ref, rt_ref, ids_ref, x_ref, g_ref, res_ref, out_ref):
    r = pl.program_id(0)
    y, z = pos[0], pos[1]
    block = lax.rem(z + r, NZ)
    cols = pl.ds(pl.multiple_of(block * TOK, TOK), TOK)
    att = att_ref[:, cols].astype(F32).T.astype(BF16)
    resid = hid_ref[0].astype(F32) + jnp.dot(att, wo_ref[...], preferred_element_type=F32)
    centered = resid - jnp.mean(resid, axis=1, keepdims=True)
    var = jnp.mean(centered * centered, axis=1, keepdims=True)
    normed = (centered * lax.rsqrt(var + 1e-06) * (1.0 + mod_ref[0:1]) + mod_ref[1:2]).astype(BF16)

    @pl.when(r == 0)
    def _():
        res_ref[...] = resid
        out_ref[...] = att

    logits = jnp.dot(normed, rt_ref[...], preferred_element_type=F32)
    logits = logits[:, 256:384] + logits[:, 128:256] + logits[:, :128]
    id0, id1 = ids_ref[0, :, 0:1], ids_ref[0, :, 1:2]
    lane = lax.broadcasted_iota(jnp.int32, (TOK, TOK), 1)
    token = lax.broadcasted_iota(jnp.int32, (TOK, TOK), 0)
    zero = jnp.zeros((TOK, TOK), F32)
    c0 = jnp.sum(jnp.where(lane == id0, logits, zero), axis=1, keepdims=True)
    c1 = jnp.sum(jnp.where(lane == id1, logits, zero), axis=1, keepdims=True)
    gate0 = jax.nn.sigmoid(c0 - c1)
    gate1 = 1.0 - gate0
    expert = ((y + lane // CAP) % NY) * NY + z // 2
    first, second = expert == id0, expert == id1
    chosen = jnp.where(first | second, 1.0, 0.0)
    earlier = jnp.where(lane < token, 1.0, 0.0).astype(BF16)
    before = jnp.dot(earlier, chosen.astype(BF16), preferred_element_type=F32)
    hit = jnp.where(before == (lane % CAP).astype(F32), chosen, zero)
    gate = hit * jnp.where(first, gate0, gate1)
    high = gate.astype(BF16)
    g_ref[0, :, :TOK] = high
    g_ref[0, :, TOK:] = (gate - high.astype(F32)).astype(BF16)
    rows = jnp.dot(hit.T.astype(BF16), normed, preferred_element_type=F32).astype(BF16)
    for e in range(NY):
        x_ref[e, 0] = rows[e * CAP : (e + 1) * CAP]


def norm_and_dispatch(pos, hid, att, w_out, modulation, router3, ids):
    whole = lambda a: pl.BlockSpec(a.shape, lambda r, pos: (0,) * a.ndim)
    turn = lambda r, pos: (lax.rem(pos[1] + r, NZ), 0, 0)
    return pl.pallas_call(
        norm_kernel,
        grid_spec=pltpu.PrefetchScalarGridSpec(
            num_scalar_prefetch=1,
            grid=(NZ,),
            in_specs=[
                pl.BlockSpec((1, TOK, D), turn),
                whole(att),
                whole(w_out),
                whole(modulation),
                whole(router3),
                pl.BlockSpec((1, TOK, 2), turn),
            ],
            out_specs=(
                pl.BlockSpec((NY, 1, CAP, D), lambda r, pos: (0, r, 0, 0)),
                pl.BlockSpec((1, TOK, 2 * TOK), lambda r, pos: (r, 0, 0)),
                pl.BlockSpec((TOK, D), lambda r, pos: (0, 0)),
                pl.BlockSpec((TOK, HD), lambda r, pos: (0, 0)),
            ),
        ),
        out_shape=(
            jax.ShapeDtypeStruct((NY, NZ, CAP, D), BF16),
            jax.ShapeDtypeStruct((NZ, TOK, 2 * TOK), BF16),
            jax.ShapeDtypeStruct((TOK, D), F32),
            jax.ShapeDtypeStruct((TOK, HD), BF16),
        ),
        compiler_params=params("arbitrary"),
        cost_estimate=pl.CostEstimate(
            flops=2 * ROW * D * (HD + 512), bytes_accessed=16 << 20, transcendentals=ROW
        ),
    )(pos, hid, att, w_out, modulation, router3, ids)


def expert_kernel(x_ref, w1_ref, w2_ref, o_ref, acc):
    j = pl.program_id(0)
    hidden = jax.nn.gelu(
        jnp.dot(x_ref[...], w1_ref[...], preferred_element_type=F32), approximate=True
    ).astype(BF16)
    term = jnp.dot(hidden, w2_ref[...], preferred_element_type=F32)

    @pl.when(j == 0)
    def _():
        acc[...] = term

    @pl.when(j > 0)
    def _():
        acc[...] += term

    @pl.when(j == pl.num_programs(0) - 1)
    def _():
        o_ref[...] = acc[...].astype(BF16)


def expert(x, w1, w2, tile=512):
    n = x.shape[0]
    return pl.pallas_call(
        expert_kernel,
        grid=(D // tile,),
        out_shape=jax.ShapeDtypeStruct((n, D), BF16),
        in_specs=[
            pl.BlockSpec((n, D), lambda j: (0, 0)),
            pl.BlockSpec((D, tile), lambda j: (0, j)),
            pl.BlockSpec((tile, D), lambda j: (j, 0)),
        ],
        out_specs=pl.BlockSpec((n, D), lambda j: (0, 0)),
        scratch_shapes=[pltpu.VMEM((n, D), F32)],
        compiler_params=params("arbitrary"),
        cost_estimate=pl.CostEstimate(
            flops=4 * n * D * D, bytes_accessed=11 << 20, transcendentals=n * D
        ),
    )(x, w1, w2)


def combine_kernel(g_ref, y0, y1, y2, y3, res_ref, part_ref, own_ref):
    r = pl.program_id(0)
    rows = jnp.concatenate([y0[0], y1[0], y2[0], y3[0]], axis=0)
    rows = jnp.concatenate([rows, rows], axis=0)
    total = jnp.dot(g_ref[0], rows, preferred_element_type=F32)
    part_ref[0] = total.astype(BF16)

    @pl.when(r == 0)
    def _():
        own_ref[...] = res_ref[...] + total


def combine(gates, ys, resid):
    block = pl.BlockSpec((1, CAP, D), lambda r: (r, 0, 0))
    own = pl.BlockSpec((TOK, D), lambda r: (0, 0))
    return pl.pallas_call(
        combine_kernel,
        grid=(NZ,),
        out_shape=(
            jax.ShapeDtypeStruct((NZ, TOK, D), BF16),
            jax.ShapeDtypeStruct((TOK, D), F32),
        ),
        in_specs=[pl.BlockSpec((1, TOK, 2 * TOK), lambda r: (r, 0, 0))] + [block] * 4 + [own],
        out_specs=(pl.BlockSpec((1, TOK, D), lambda r: (r, 0, 0)), own),
        compiler_params=params("arbitrary"),
        cost_estimate=pl.CostEstimate(
            flops=4 * ROW * TOK * D, bytes_accessed=8 << 20, transcendentals=0
        ),
    )(gates, *ys, resid)


def send(x, axis, n, shift):
    return lax.ppermute(x, axis, [(i, (i + shift) % n) for i in range(n)])


def after(x, *done):
    return lax.optimization_barrier((x,) + done)[0]


def gather_z(x):
    return lax.all_gather(x, "z", axis=0, tiled=False)


def gather_rows_z(x):
    z = lax.axis_index("z")
    out = jnp.zeros((NZ,) + x.shape, x.dtype)
    place = lambda out, block, at: lax.dynamic_update_slice(out, block[None], (at % NZ, 0, 0))
    out = place(out, x, z)
    up, down = x, x
    for s in range(1, 4):
        up, down = send(up, "z", NZ, 1), send(down, "z", NZ, -1)
        out = place(out, up, z + NZ - s)
        out = place(out, down, z + s)
    half = x.shape[0] // 2
    up, down = send(up[:half], "z", NZ, 1), send(down[half:], "z", NZ, -1)
    return place(out, jnp.concatenate([up, down], axis=0), z + 4)


def scatter_sum_z(parts, own):
    half = TOK // 2
    down, up = send(parts[4][:half], "z", NZ, -1), send(parts[4][half:], "z", NZ, 1)
    add = lambda a, b: (a.astype(F32) + b.astype(F32)).astype(BF16)
    down = jnp.concatenate([add(parts[5][:half], down), parts[5][half:]], axis=0)
    up = jnp.concatenate([parts[3][:half], add(parts[3][half:], up)], axis=0)
    for s in (6, 7):
        down, up = send(down, "z", NZ, -1), send(up, "z", NZ, 1)
        down, up = add(parts[s], down), add(parts[NZ - s], up)
    down, up = send(down, "z", NZ, -1), send(up, "z", NZ, 1)
    return (own + down.astype(F32) + up.astype(F32)).astype(BF16)


def per_device(
    hidden_in, queries, fresh_kv, stale_kv, modulation, w_out, router, fc_in, fc_out, expert_ids
):
    y, z = lax.axis_index("y"), lax.axis_index("z")
    pos = jnp.stack([y, z]).astype(jnp.int32)
    batch = lax.axis_size("batch")

    def neighbour(w):
        rows = D // batch
        part = lax.dynamic_slice_in_dim(w, lax.axis_index("batch") * rows, rows, 0)
        return lax.all_gather(send(part, "y", NY, -1), "batch", axis=0, tiled=True)

    w1, w2 = fc_in[0], fc_out[0]
    w1_next, w2_next = neighbour(w1), neighbour(w2)

    kv = lax.all_to_all(split_heads(stale_kv), "z", split_axis=0, concat_axis=0, tiled=True)
    qf = lax.all_to_all(
        split_heads(after(queries, kv), fresh_kv), "z", split_axis=0, concat_axis=0, tiled=True
    )
    ids = gather_z(after(expert_ids, kv))
    hid = gather_z(after(hidden_in, kv))
    kv_prev, kv_next = send(kv, "y", NY, 1), send(kv, "y", NY, -1)
    kv_far = [send(kv_prev[:4], "y", NY, 1), send(kv_next[4:], "y", NY, -1)]
    q, m, l, acc = attend_own_row(qf, kv)
    m, l, acc = attend_other_rows([kv_prev, kv_next], (q, m, l, acc), False)
    (att,) = attend_other_rows([jnp.concatenate(kv_far, axis=0)], (q, m, l, acc), True)
    att = gather_rows_z(att).reshape(HD, ROW)

    pieces, rest = [], router
    for _ in range(3):
        piece = lax.reduce_precision(rest, exponent_bits=8, mantissa_bits=7)
        rest = rest - piece
        pieces.append(jnp.pad(piece.astype(BF16), ((0, 0), (0, TOK - EXPERTS))))
    router3 = jnp.concatenate(pieces, axis=1)
    x, gates, resid, attended = norm_and_dispatch(
        pos, hid, att, w_out, modulation, router3, ids
    )
    x = [x[e].reshape(NZ * CAP, D) for e in range(NY)]

    x_prev, x_next = send(x[2], "y", NY, 1), send(x[3], "y", NY, -1)
    y0 = expert(x[0], w1, w2)
    y3 = send(expert(x_next, w1, w2), "y", NY, 1)
    y1 = expert(x[1], w1_next, w2_next)
    y2 = send(expert(x_prev, w1_next, w2_next), "y", NY, -1)
    ys = [a.reshape(NZ, CAP, D) for a in (y0, y1, y2, y3)]
    parts, own = combine(gates, ys, resid)
    return attended, scatter_sum_z(parts, own)


def solution(mesh):
    split = Mesh(mesh.devices.reshape(NY, NZ, -1), ("y", "z", "batch"))
    tokens = P(("batch", "y", "z"), None)
    return jax.shard_map(
        per_device,
        mesh=split,
        in_specs=(
            tokens,
            tokens,
            tokens,
            tokens,
            P("batch", None),
            P(),
            P(),
            P(("y", "z"), None, None),
            P(("y", "z"), None, None),
            tokens,
        ),
        out_specs=(tokens, tokens),
        check_vma=False,
    )
```

time: 389 us -> 272 us (0.70)
  waiting for transfers between devices: 191 us -> 85.7 us
  Pallas kernels: 0 us -> 62.1 us
  starting transfers between devices: 5.2 us -> 50.7 us
  blocking collectives: 78.9 us -> 39.2 us
  matrix products: 37.9 us -> 0 us
  local copies, waits for them, and re-layouts: 48.8 us -> 14.5 us
  other arithmetic: 12.3 us -> 5.38 us
    all_gather x1 -> x3, waiting for transfers between devices: 121 us -> 0.02 us  [the longest x1 0.02 us: gather_z(): return lax.all_gather(x, 'z', axis=0, tiled=False)]
    ppermute x0 -> x26, waiting for transfers between devices: none -> 85.6 us  [send(): return lax.ppermute(x, axis, [(i, (i + shift) % n) for i in range(n)])]
    all_to_all x1, waiting for transfers between devices: 69.8 us -> 0.01 us  [per_device(): lax.all_to_all(split_heads(after(queries, kv), fresh_kv), 'z', split_axis...]
    pallas_call x0 -> x11, Pallas kernels: none -> 62.1 us  [the longest x4 26.6 us: expert(): pl.pallas_call(expert_kernel, grid=(D // tile,), out_shape=jax.ShapeDtype...]
    all_to_all x1, blocking collectives: 78.9 us -> 22.9 us  [per_device(): lax.all_to_all(split_heads(stale_kv), 'z', split_axis=0, concat_axis=0, t...]
    ppermute x0 -> x26, starting transfers between devices: none -> 46.5 us  [send(): return lax.ppermute(x, axis, [(i, (i + shift) % n) for i in range(n)])]
    dot_general x5 -> x0, matrix products: 26.4 us -> none  [the longest x1 10.2 us: attend_block(): jnp.einsum('hqk,khd->qhd', weights, vh, preferred_element_type=jnp.float32)]
    slice x4 -> x6, local copies, waits for them, and re-layouts: 27.9 us -> 3.77 us  [the longest x1 2.31 us: per_device(): x = [x[e].reshape(NZ * CAP, D) for e in range(NY)]]
  transfers between devices with their start and end apart: 2 -> 30, of which waited for: 2 -> 14; matrix products, arithmetic and copies ran while one was open for 2% -> 4% of each run, Pallas kernels for 0% -> 21%
where the time goes in v1:
time: 272 us
  waiting for transfers between devices  85.7 us (32%)
  Pallas kernels  62.1 us (23%)
  starting transfers between devices  50.7 us (19%)
  blocking collectives  39.2 us (14%)
  local copies, waits for them, and re-layouts  14.5 us (5%)
  between operations  14.3 us (5%)
  other arithmetic  5.38 us (2%)
    ppermute x26, waiting for transfers between devices, send(): return lax.ppermute(x, axis, [(i, (i + shift) % n) for i in range(n)])  85.6 us
    ppermute x26, starting transfers between devices, send(): return lax.ppermute(x, axis, [(i, (i + shift) % n) for i in range(n)])  46.5 us
    pallas_call x4, Pallas kernels, expert(): pl.pallas_call(expert_kernel, grid=(D // tile,), out_shape=jax.ShapeDtype...  26.6 us
    all_to_all x1, blocking collectives, per_device(): lax.all_to_all(split_heads(stale_kv), 'z', split_axis=0, concat_axis=0, t...  22.9 us
    all_gather x1, blocking collectives, gather_z(): return lax.all_gather(x, 'z', axis=0, tiled=False)  16.2 us
    pallas_call x1, Pallas kernels, norm_and_dispatch(): pl.pallas_call(norm_kernel, grid_spec=pltpu.PrefetchScalarGridSpec(num_sc...  15.5 us
    pallas_call x2, Pallas kernels, attend_other_rows(): pl.pallas_call(functools.partial(other_rows_kernel, last, tile, n), grid=...  9.11 us
    unnamed x29, local copies, waits for them, and re-layouts  5.96 us
  transfers between devices with their start and end apart: 30, of which 14 were waited for; matrix products, arithmetic and copies ran while one was open for 4% of the time, Pallas kernels for 21%

profile of v1, /device:TPU:2, one launch (start us, length us, event | category | flops | bytes accessed | tf_op | source)
XLA Modules:
  0.0 271.8 jit_solution(5319095193700069434)
XLA Ops:
  8.4 22.9 %all_to_all.10.kv_ref = bf16[8,192,128]{2,1,0:T(8,128)(2,1)S(1)} all-to-all(bf16[8,192,128]{2,1,0:T(8,128)(2,1)S(1)} %shard_map.113), channel_id=1, replica_groups=mesh['y'=4,'z'=8,'batch'=8] {'z'}, dimensions={0} | all-to-all | bytes 786432 | tf_op jit(solution)/shard_map/all_to_all | solution.py:361
  35.7 11.1 %collective-permute-done.12 = bf16[192,1536]{1,0:T(8,128)(2,1)S(1)} collective-permute-done((bf16[192,1536]{1,0:T(8,128)(2,1)S(1)}, bf16[192,1536]{1,0:T(8,128)(2,1)S(1)}, u32[]{:S(2)}, u32[]{:S(2)}) %collective-permute-start.12) | collective-permute-done | bytes 589856 | tf_op jit(solution)/shard_map/ppermute | solution.py:307
  48.8 3.8 %collective-permute-start.13 = (bf16[192,1536]{1,0:T(8,128)(2,1)S(1)}, bf16[192,1536]{1,0:T(8,128)(2,1)S(1)}, u32[]{:S(2)}, u32[]{:S(2)}) collective-permute-start(bf16[192,1536]{1,0:T(8,128)(2,1)S(1)} %dynamic-slice_bitcast_fusion), channel_id=1, source_target_pairs={{0,192},{64,0},{128,64},{192,128},{1,193},{65,1},{129,65},{193,129... | collective-permute-start | bytes 1769480 | tf_op jit(solution)/shard_map/ppermute | solution.py:307
  52.6 10.3 %collective-permute-done.13 = bf16[192,1536]{1,0:T(8,128)(2,1)S(1)} collective-permute-done((bf16[192,1536]{1,0:T(8,128)(2,1)S(1)}, bf16[192,1536]{1,0:T(8,128)(2,1)S(1)}, u32[]{:S(2)}, u32[]{:S(2)}) %collective-permute-start.13) | collective-permute-done | bytes 589856 | tf_op jit(solution)/shard_map/ppermute | solution.py:307
  66.3 4.0 %all-to-all-start.1 = ((bf16[8,288,128]{2,1,0:T(8,128)(2,1)}), bf16[8,288,128]{2,1,0:T(8,128)(2,1)S(1)}, u32[]{:S(2)}, u32[]{:S(2)}) async-start(bf16[8,288,128]{2,1,0:T(8,128)(2,1)} %shard_map.114), calls=%async_computation.1 | async-start | bytes 1179648 | tf_op jit(solution)/shard_map/all_to_all | solution.py:362
  70.3 3.8 %collective-permute-start.2 = (bf16[8,192,128]{2,1,0:T(8,128)(2,1)S(1)}, bf16[8,192,128]{2,1,0:T(8,128)(2,1)S(1)}, u32[]{:S(2)}, u32[]{:S(2)}) collective-permute-start(bf16[8,192,128]{2,1,0:T(8,128)(2,1)S(1)} %all_to_all.10.kv_ref), channel_id=1, source_target_pairs={{0,192},{64,0},{128,64},{192,128},{1,193},{65,1},{129,65},{193,129... | collective-permute-start | bytes 1179656 | tf_op jit(solution)/shard_map/ppermute | solution.py:307
  75.6 5.2 %collective-permute-done.refs_0_ = bf16[8,192,128]{2,1,0:T(8,128)(2,1)S(1)} collective-permute-done((bf16[8,192,128]{2,1,0:T(8,128)(2,1)S(1)}, bf16[8,192,128]{2,1,0:T(8,128)(2,1)S(1)}, u32[]{:S(2)}, u32[]{:S(2)}) %collective-permute-start) | collective-permute-done | bytes 393248 | tf_op jit(solution)/shard_map/ppermute | solution.py:307
  84.7 16.2 %all-gather.1 = s32[1024,2]{0,1:T(2,128)S(1)} all-gather(s32[128,2]{0,1:T(2,128)S(1)} %copy-done.13), channel_id=3, replica_groups=mesh['y'=4,'z'=8,'batch'=8] {'z'}, dimensions={0}, use_global_device_ids=true | all-gather | bytes 9216 | tf_op jit(solution)/shard_map/all_gather | solution.py:315
  103.1 5.1 %shard_map.115 = (bf16[1024,96]{1,0:T(8,128)(2,1)S(1)}, f32[1024,1]{1,0:T(8,128)S(1)}, f32[1024,1]{1,0:T(8,128)S(1)}, f32[1024,96]{1,0:T(8,128)S(1)}) custom-call(bf16[8,288,128]{2,1,0:T(8,128)(2,1)S(1)} %all-to-all-done.1.qf_ref, bf16[8,192,128]{2,1,0:T(8,128)(2,1)S(1)} %all_to_all.10.kv_ref), custom_call_target="tpu_custom_call" | custom-call | flops 402653184 | bytes 4194304 | tf_op jit(solution)/shard_map/pallas_call | solution.py:77
  108.2 5.2 %shard_map.116 = (f32[1024,1]{1,0:T(8,128)S(1)}, f32[1024,1]{1,0:T(8,128)S(1)}, f32[1024,96]{1,0:T(8,128)S(1)}) custom-call(bf16[8,192,128]{2,1,0:T(8,128)(2,1)S(1)} %collective-permute-done.refs_0_, bf16[8,192,128]{2,1,0:T(8,128)(2,1)S(1)} %collective-permute-done.2.refs_1_, bf16[1024,96]{1,0:T(8,128)(2,1)S(1)} %get-tuple-element.20.refs_2_.refs_1_, ...), custom_call_target="tpu_custom_call" | custom-call | flops 805306368 | bytes 5242880 | tf_op jit(solution)/shard_map/pallas_call | solution.py:143
  113.4 3.9 %shard_map.117 = bf16[96,1024]{1,0:T(8,128)(2,1)S(1)} custom-call(bf16[8,192,128]{2,1,0:T(8,128)(2,1)S(1)} %pad_maximum_fusion.refs_0_, bf16[1024,96]{1,0:T(8,128)(2,1)S(1)} %get-tuple-element.20.refs_2_.refs_1_, f32[1024,1]{1,0:T(8,128)S(1)} %get-tuple-element.24.refs_2_, f32[1024,1]{1,0:T(8,128)S(1)} %get-tuple-element.25.refs_3_, ...), custom_call_target="tpu_custom_call" | custom-call | flops 402653184 | bytes 5242880 | tf_op jit(solution)/shard_map/pallas_call | solution.py:143
  120.9 3.4 %collective-permute-done.4 = bf16[96,1024]{1,0:T(8,128)(2,1)S(1)} collective-permute-done((bf16[96,1024]{1,0:T(8,128)(2,1)S(1)}, bf16[96,1024]{1,0:T(8,128)(2,1)S(1)}, u32[]{:S(2)}, u32[]{:S(2)}) %collective-permute-start.4) | collective-permute-done | bytes 196640 | tf_op jit(solution)/shard_map/ppermute | solution.py:307
  127.6 3.7 %collective-permute-done.6 = bf16[96,1024]{1,0:T(8,128)(2,1)S(1)} collective-permute-done((bf16[96,1024]{1,0:T(8,128)(2,1)S(1)}, bf16[96,1024]{1,0:T(8,128)(2,1)S(1)}, u32[]{:S(2)}, u32[]{:S(2)}) %collective-permute-start.6) | collective-permute-done | bytes 196640 | tf_op jit(solution)/shard_map/ppermute | solution.py:307
  131.3 3.4 %collective-permute-start.9 = (bf16[96,1024]{1,0:T(8,128)(2,1)S(1)}, bf16[96,1024]{1,0:T(8,128)(2,1)S(1)}, u32[]{:S(2)}, u32[]{:S(2)}) collective-permute-start(bf16[96,1024]{1,0:T(8,128)(2,1)S(1)} %collective-permute-done.7), channel_id=1, source_target_pairs={{0,56},{8,0},{16,8},{24,16},{32,24},{40,32},{48,40},{56,48},{1,57}... | collective-permute-start | bytes 589832 | tf_op jit(solution)/shard_map/ppermute | solution.py:307
  134.8 3.4 %collective-permute-done.8 = bf16[96,1024]{1,0:T(8,128)(2,1)S(1)} collective-permute-done((bf16[96,1024]{1,0:T(8,128)(2,1)S(1)}, bf16[96,1024]{1,0:T(8,128)(2,1)S(1)}, u32[]{:S(2)}, u32[]{:S(2)}) %collective-permute-start.8) | collective-permute-done | bytes 196640 | tf_op jit(solution)/shard_map/ppermute | solution.py:307
  138.3 3.4 %collective-permute-start.11 = (bf16[48,1024]{1,0:T(8,128)(2,1)S(1)}, bf16[48,1024]{1,0:T(8,128)(2,1)S(1)}, u32[]{:S(2)}, u32[]{:S(2)}) collective-permute-start(bf16[48,1024]{1,0:T(8,128)(2,1)S(1)} %slice.105), channel_id=1, source_target_pairs={{0,56},{8,0},{16,8},{24,16},{32,24},{40,32},{48,40},{56,48},{1,57}... | collective-permute-start | bytes 294920 | tf_op jit(solution)/shard_map/ppermute | solution.py:307
  145.2 15.5 %shard_map.118 = (bf16[4,8,32,1536]{3,2,1,0:T(8,128)(2,1)}, bf16[8,128,256]{2,1,0:T(8,128)(2,1)S(1)}, f32[128,1536]{1,0:T(8,128)S(1)}, bf16[128,768]{1,0:T(8,128)(2,1)}) custom-call(s32[2]{0:T(128)S(1)} %pad_add_fusion.pos, bf16[8,128,1536]{2,1,0:T(8,128)(2,1)} %bitcast.77, bf16[768,1024]{1,0:T(8,128)(2,1)S(1)} %bitcast.67, bf16[768,1536]{1,0:T(8,128)(2,1)} %wo_ref.1, ...), custom_call_target="tpu_custom_call" | custom-call | flops 4026531840 | bytes 16777216 | tf_op jit(solution)/shard_map/pallas_call | solution.py:202
  165.2 10.0 %collective-permute-done.16.x_ref = bf16[256,1536]{1,0:T(8,128)(2,1)S(1)} collective-permute-done((bf16[256,1536]{1,0:T(8,128)(2,1)S(1)}, bf16[256,1536]{1,0:T(8,128)(2,1)S(1)}, u32[]{:S(2)}, u32[]{:S(2)}) %collective-permute-start.16) | collective-permute-done | bytes 786464 | tf_op jit(solution)/shard_map/ppermute | solution.py:307
  175.1 7.3 %shard_map.122 = bf16[256,1536]{1,0:T(8,128)(2,1)} custom-call(bf16[256,1536]{1,0:T(8,128)(2,1)S(1)} %collective-permute-done.16.x_ref, bf16[1536,1536]{1,0:T(8,128)(2,1)} %bitcast.71, bf16[1536,1536]{1,0:T(8,128)(2,1)} %bitcast.73), custom_call_target="tpu_custom_call" | custom-call | flops 2415919104 | bytes 11534336 | tf_op jit(solution)/shard_map/pallas_call | solution.py:257
  184.4 6.4 %shard_map.121 = bf16[256,1536]{1,0:T(8,128)(2,1)S(1)} custom-call(bf16[256,1536]{1,0:T(8,128)(2,1)S(1)} %copy-done.1, bf16[1536,1536]{1,0:T(8,128)(2,1)} %all-gather.6.cloned.1.call-done.w1_ref, bf16[1536,1536]{1,0:T(8,128)(2,1)} %all-gather.8.cloned.1.call-done.w2_ref), custom_call_target="tpu_custom_call" | custom-call | flops 2415919104 | bytes 11534336 | tf_op jit(solution)/shard_map/pallas_call | solution.py:257
  190.9 3.5 %collective-permute-start.15 = (bf16[256,1536]{1,0:T(8,128)(2,1)S(1)}, bf16[256,1536]{1,0:T(8,128)(2,1)S(1)}, u32[]{:S(2)}, u32[]{:S(2)}) collective-permute-start(bf16[256,1536]{1,0:T(8,128)(2,1)S(1)} %shard_map.121), channel_id=1, source_target_pairs={{0,192},{64,0},{128,64},{192,128},{1,193},{65,1},{129,65},{193,129... | collective-permute-start | bytes 2359304 | tf_op jit(solution)/shard_map/ppermute | solution.py:307
  194.4 6.4 %shard_map.119 = bf16[256,1536]{1,0:T(8,128)(2,1)S(1)} custom-call(bf16[256,1536]{1,0:T(8,128)(2,1)S(1)} %bitcast.64, bf16[1536,1536]{1,0:T(8,128)(2,1)} %bitcast.72, bf16[1536,1536]{1,0:T(8,128)(2,1)} %bitcast.74), custom_call_target="tpu_custom_call" | custom-call | flops 2415919104 | bytes 11534336 | tf_op jit(solution)/shard_map/pallas_call | solution.py:257
  200.8 6.5 %shard_map.120 = bf16[256,1536]{1,0:T(8,128)(2,1)S(1)} custom-call(bf16[256,1536]{1,0:T(8,128)(2,1)S(1)} %bitcast.63, bf16[1536,1536]{1,0:T(8,128)(2,1)} %all-gather.6.cloned.1.call-done.w1_ref, bf16[1536,1536]{1,0:T(8,128)(2,1)} %all-gather.8.cloned.1.call-done.w2_ref), custom_call_target="tpu_custom_call" | custom-call | flops 2415919104 | bytes 11534336 | tf_op jit(solution)/shard_map/pallas_call | solution.py:257
  207.4 4.5 %shard_map.123 = (bf16[8,128,1536]{2,1,0:T(8,128)(2,1)}, f32[128,1536]{1,0:T(8,128)S(1)}) custom-call(bf16[8,128,256]{2,1,0:T(8,128)(2,1)S(1)} %copy-done.3, bf16[8,32,1536]{2,1,0:T(8,128)(2,1)S(1)} %bitcast.65, bf16[8,32,1536]{2,1,0:T(8,128)(2,1)S(1)} %bitcast.66, bf16[8,32,1536]{2,1,0:T(8,128)(2,1)S(1)} %bitcast.69, bf16[8,32,1536]{2,1,0:T(8,128)(2,1)S(1)} %bitcast.68, ...), custom_call_target="tpu_custom_call" | custom-call | flops 805306368 | bytes 8388608 | tf_op jit(solution)/shard_map/pallas_call | solution.py:290
  213.3 3.5 %collective-permute-start.18 = (bf16[64,1536]{1,0:T(8,128)(2,1)S(1)}, bf16[64,1536]{1,0:T(8,128)(2,1)S(1)}, u32[]{:S(2)}, u32[]{:S(2)}) collective-permute-start(bf16[64,1536]{1,0:T(8,128)(2,1)S(1)} %get-tuple-element.38), channel_id=1, source_target_pairs={{0,56},{8,0},{16,8},{24,16},{32,24},{40,32},{48,40},{56,48},{1,57}... | collective-permute-start | bytes 589832 | tf_op jit(solution)/shard_map/ppermute | solution.py:307
  216.8 5.2 %collective-permute-done.18 = bf16[64,1536]{1,0:T(8,128)(2,1)S(1)} collective-permute-done((bf16[64,1536]{1,0:T(8,128)(2,1)S(1)}, bf16[64,1536]{1,0:T(8,128)(2,1)S(1)}, u32[]{:S(2)}, u32[]{:S(2)}) %collective-permute-start.18) | collective-permute-done | bytes 196640 | tf_op jit(solution)/shard_map/ppermute | solution.py:307
  227.1 9.2 %collective-permute-done.19 = bf16[128,1536]{1,0:T(8,128)(2,1)S(1)} collective-permute-done((bf16[128,1536]{1,0:T(8,128)(2,1)S(1)}, bf16[128,1536]{1,0:T(8,128)(2,1)S(1)}, u32[]{:S(2)}, u32[]{:S(2)}) %collective-permute-start.19) | collective-permute-done | bytes 393248 | tf_op jit(solution)/shard_map/ppermute | solution.py:307
  236.4 3.8 %collective-permute-start.20 = (bf16[128,1536]{1,0:T(8,128)(2,1)S(1)}, bf16[128,1536]{1,0:T(8,128)(2,1)S(1)}, u32[]{:S(2)}, u32[]{:S(2)}) collective-permute-start(bf16[128,1536]{1,0:T(8,128)(2,1)S(1)} %fusion.10), channel_id=1, source_target_pairs={{0,56},{8,0},{16,8},{24,16},{32,24},{40,32},{48,40},{56,48},{1,57}... | collective-permute-start | bytes 1179656 | tf_op jit(solution)/shard_map/ppermute | solution.py:307
  240.2 5.3 %collective-permute-done.20 = bf16[128,1536]{1,0:T(8,128)(2,1)S(1)} collective-permute-done((bf16[128,1536]{1,0:T(8,128)(2,1)S(1)}, bf16[128,1536]{1,0:T(8,128)(2,1)S(1)}, u32[]{:S(2)}, u32[]{:S(2)}) %collective-permute-start.20) | collective-permute-done | bytes 393248 | tf_op jit(solution)/shard_map/ppermute | solution.py:307
  245.8 3.8 %collective-permute-start.21 = (bf16[128,1536]{1,0:T(8,128)(2,1)S(1)}, bf16[128,1536]{1,0:T(8,128)(2,1)S(1)}, u32[]{:S(2)}, u32[]{:S(2)}) collective-permute-start(bf16[128,1536]{1,0:T(8,128)(2,1)S(1)} %get-tuple-element.34), channel_id=1, source_target_pairs={{0,56},{8,0},{16,8},{24,16},{32,24},{40,32},{48,40},{56,48},{1,57}... | collective-permute-start | bytes 1179656 | tf_op jit(solution)/shard_map/ppermute | solution.py:307
  249.5 5.7 %collective-permute-done.24 = bf16[128,1536]{1,0:T(8,128)(2,1)S(1)} collective-permute-done((bf16[128,1536]{1,0:T(8,128)(2,1)S(1)}, bf16[128,1536]{1,0:T(8,128)(2,1)S(1)}, u32[]{:S(2)}, u32[]{:S(2)}) %collective-permute-start.24) | collective-permute-done | bytes 393248 | tf_op jit(solution)/shard_map/ppermute | solution.py:307
  255.4 9.0 %collective-permute-done.25 = bf16[128,1536]{1,0:T(8,128)(2,1)S(1)} collective-permute-done((bf16[128,1536]{1,0:T(8,128)(2,1)S(1)}, bf16[128,1536]{1,0:T(8,128)(2,1)S(1)}, u32[]{:S(2)}, u32[]{:S(2)}) %collective-permute-start.25) | collective-permute-done | bytes 393248 | tf_op jit(solution)/shard_map/ppermute | solution.py:307
  (104 shorter events, 42.9 us)
Async XLA Ops:
  7.2 137.0 %all-gather.10.cloned.1.call-start = ((), (), s32[]{:S(2)}) async-start(), calls=%async_computation.4 | async-start | bytes 3538944 | tf_op jit(solution)/shard_map/all_gather | solution.py:315
  31.4 151.9 %all-gather.6.cloned.1.call-start = ((), (), s32[]{:S(2)}) async-start(), calls=%async_computation.2 | async-start | bytes 5308416 | tf_op jit(solution)/shard_map/all_gather | solution.py:356
  31.4 32.4 %copy-start.12 = (f32[1536,16]{0,1:T(8,128)S(1)}, f32[1536,16]{0,1:T(8,128)}, u32[]{:S(2)}) copy-start(f32[1536,16]{0,1:T(8,128)} %param.16) | copy-start | bytes 294916
  32.6 14.2 %collective-permute-start.12 = (bf16[192,1536]{1,0:T(8,128)(2,1)S(1)}, bf16[192,1536]{1,0:T(8,128)(2,1)S(1)}, u32[]{:S(2)}, u32[]{:S(2)}) collective-permute-start(bf16[192,1536]{1,0:T(8,128)(2,1)S(1)} %dynamic-slice_bitcast_fusion.1), channel_id=1, source_target_pairs={{0,192},{64,0},{128,64},{192,128},{1,193},{65,1},{129,65},{193,129... | collective-permute-start | bytes 1769480 | tf_op jit(solution)/shard_map/ppermute | solution.py:307
  47.6 135.7 %all-gather.8.cloned.1.call-start = ((), (), s32[]{:S(2)}) async-start(), calls=%async_computation.3 | async-start | bytes 5308416 | tf_op jit(solution)/shard_map/all_gather | solution.py:356
  48.8 14.1 %collective-permute-start.13 = (bf16[192,1536]{1,0:T(8,128)(2,1)S(1)}, bf16[192,1536]{1,0:T(8,128)(2,1)S(1)}, u32[]{:S(2)}, u32[]{:S(2)}) collective-permute-start(bf16[192,1536]{1,0:T(8,128)(2,1)S(1)} %dynamic-slice_bitcast_fusion), channel_id=1, source_target_pairs={{0,192},{64,0},{128,64},{192,128},{1,193},{65,1},{129,65},{193,129... | collective-permute-start | bytes 1769480 | tf_op jit(solution)/shard_map/ppermute | solution.py:307
  66.3 36.8 %all-to-all-start.1 = ((bf16[8,288,128]{2,1,0:T(8,128)(2,1)}), bf16[8,288,128]{2,1,0:T(8,128)(2,1)S(1)}, u32[]{:S(2)}, u32[]{:S(2)}) async-start(bf16[8,288,128]{2,1,0:T(8,128)(2,1)} %shard_map.114), calls=%async_computation.1 | async-start | bytes 1179648 | tf_op jit(solution)/shard_map/all_to_all | solution.py:362
  70.3 10.5 %collective-permute-start = (bf16[8,192,128]{2,1,0:T(8,128)(2,1)S(1)}, bf16[8,192,128]{2,1,0:T(8,128)(2,1)S(1)}, u32[]{:S(2)}, u32[]{:S(2)}) collective-permute-start(bf16[8,192,128]{2,1,0:T(8,128)(2,1)S(1)} %all_to_all.10.kv_ref), channel_id=1, source_target_pairs={{0,64},{64,128},{128,192},{192,0},{1,65},{65,129},{129,193},{193,1... | collective-permute-start | bytes 1179656 | tf_op jit(solution)/shard_map/ppermute | solution.py:307
  70.3 10.7 %collective-permute-start.2 = (bf16[8,192,128]{2,1,0:T(8,128)(2,1)S(1)}, bf16[8,192,128]{2,1,0:T(8,128)(2,1)S(1)}, u32[]{:S(2)}, u32[]{:S(2)}) collective-permute-start(bf16[8,192,128]{2,1,0:T(8,128)(2,1)S(1)} %all_to_all.10.kv_ref), channel_id=1, source_target_pairs={{0,192},{64,0},{128,64},{192,128},{1,193},{65,1},{129,65},{193,129... | collective-permute-start | bytes 1179656 | tf_op jit(solution)/shard_map/ppermute | solution.py:307
  80.9 21.1 %collective-permute-start.1 = (bf16[4,192,128]{2,1,0:T(8,128)(2,1)S(1)}, bf16[4,192,128]{2,1,0:T(8,128)(2,1)}, u32[]{:S(2)}, u32[]{:S(2)}) collective-permute-start(bf16[4,192,128]{2,1,0:T(8,128)(2,1)S(1)} %slice.102), channel_id=1, source_target_pairs={{0,64},{64,128},{128,192},{192,0},{1,65},{65,129},{129,193},{193,1... | collective-permute-start | bytes 589832 | tf_op jit(solution)/shard_map/ppermute | solution.py:307
  81.0 21.0 %collective-permute-start.3 = (bf16[4,192,128]{2,1,0:T(8,128)(2,1)S(1)}, bf16[4,192,128]{2,1,0:T(8,128)(2,1)}, u32[]{:S(2)}, u32[]{:S(2)}) collective-permute-start(bf16[4,192,128]{2,1,0:T(8,128)(2,1)S(1)} %slice.103), channel_id=1, source_target_pairs={{0,192},{64,0},{128,64},{192,128},{1,193},{65,1},{129,65},{193,129... | collective-permute-start | bytes 589832 | tf_op jit(solution)/shard_map/ppermute | solution.py:307
  117.3 7.0 %collective-permute-start.4 = (bf16[96,1024]{1,0:T(8,128)(2,1)S(1)}, bf16[96,1024]{1,0:T(8,128)(2,1)S(1)}, u32[]{:S(2)}, u32[]{:S(2)}) collective-permute-start(bf16[96,1024]{1,0:T(8,128)(2,1)S(1)} %shard_map.117), channel_id=1, source_target_pairs={{0,8},{8,16},{16,24},{24,32},{32,40},{40,48},{48,56},{56,0},{1,9},... | collective-permute-start | bytes 589832 | tf_op jit(solution)/shard_map/ppermute | solution.py:307
  117.6 6.6 %collective-permute-start.5 = (bf16[96,1024]{1,0:T(8,128)(2,1)S(1)}, bf16[96,1024]{1,0:T(8,128)(2,1)S(1)}, u32[]{:S(2)}, u32[]{:S(2)}) collective-permute-start(bf16[96,1024]{1,0:T(8,128)(2,1)S(1)} %shard_map.117), channel_id=1, source_target_pairs={{0,56},{8,0},{16,8},{24,16},{32,24},{40,32},{48,40},{56,48},{1,57}... | collective-permute-start | bytes 589832 | tf_op jit(solution)/shard_map/ppermute | solution.py:307
  124.3 7.0 %collective-permute-start.6 = (bf16[96,1024]{1,0:T(8,128)(2,1)S(1)}, bf16[96,1024]{1,0:T(8,128)(2,1)S(1)}, u32[]{:S(2)}, u32[]{:S(2)}) collective-permute-start(bf16[96,1024]{1,0:T(8,128)(2,1)S(1)} %collective-permute-done.4), channel_id=1, source_target_pairs={{0,8},{8,16},{16,24},{24,32},{32,40},{40,48},{48,56},{56,0},{1,9},... | collective-permute-start | bytes 589832 | tf_op jit(solution)/shard_map/ppermute | solution.py:307
  124.3 7.0 %collective-permute-start.7 = (bf16[96,1024]{1,0:T(8,128)(2,1)S(1)}, bf16[96,1024]{1,0:T(8,128)(2,1)S(1)}, u32[]{:S(2)}, u32[]{:S(2)}) collective-permute-start(bf16[96,1024]{1,0:T(8,128)(2,1)S(1)} %collective-permute-done.5), channel_id=1, source_target_pairs={{0,56},{8,0},{16,8},{24,16},{32,24},{40,32},{48,40},{56,48},{1,57}... | collective-permute-start | bytes 589832 | tf_op jit(solution)/shard_map/ppermute | solution.py:307
  131.3 6.9 %collective-permute-start.8 = (bf16[96,1024]{1,0:T(8,128)(2,1)S(1)}, bf16[96,1024]{1,0:T(8,128)(2,1)S(1)}, u32[]{:S(2)}, u32[]{:S(2)}) collective-permute-start(bf16[96,1024]{1,0:T(8,128)(2,1)S(1)} %collective-permute-done.6), channel_id=1, source_target_pairs={{0,8},{8,16},{16,24},{24,32},{32,40},{40,48},{48,56},{56,0},{1,9},... | collective-permute-start | bytes 589832 | tf_op jit(solution)/shard_map/ppermute | solution.py:307
  131.3 7.0 %collective-permute-start.9 = (bf16[96,1024]{1,0:T(8,128)(2,1)S(1)}, bf16[96,1024]{1,0:T(8,128)(2,1)S(1)}, u32[]{:S(2)}, u32[]{:S(2)}) collective-permute-start(bf16[96,1024]{1,0:T(8,128)(2,1)S(1)} %collective-permute-done.7), channel_id=1, source_target_pairs={{0,56},{8,0},{16,8},{24,16},{32,24},{40,32},{48,40},{56,48},{1,57}... | collective-permute-start | bytes 589832 | tf_op jit(solution)/shard_map/ppermute | solution.py:307
  138.2 5.9 %collective-permute-start.10 = (bf16[48,1024]{1,0:T(8,128)(2,1)S(1)}, bf16[48,1024]{1,0:T(8,128)(2,1)S(1)}, u32[]{:S(2)}, u32[]{:S(2)}) collective-permute-start(bf16[48,1024]{1,0:T(8,128)(2,1)S(1)} %slice.104), channel_id=1, source_target_pairs={{0,8},{8,16},{16,24},{24,32},{32,40},{40,48},{48,56},{56,0},{1,9},... | collective-permute-start | bytes 294920 | tf_op jit(solution)/shard_map/ppermute | solution.py:307
  138.3 5.8 %collective-permute-start.11 = (bf16[48,1024]{1,0:T(8,128)(2,1)S(1)}, bf16[48,1024]{1,0:T(8,128)(2,1)S(1)}, u32[]{:S(2)}, u32[]{:S(2)}) collective-permute-start(bf16[48,1024]{1,0:T(8,128)(2,1)S(1)} %slice.105), channel_id=1, source_target_pairs={{0,56},{8,0},{16,8},{24,16},{32,24},{40,32},{48,40},{56,48},{1,57}... | collective-permute-start | bytes 294920 | tf_op jit(solution)/shard_map/ppermute | solution.py:307
  163.1 12.1 %collective-permute-start.16 = (bf16[256,1536]{1,0:T(8,128)(2,1)S(1)}, bf16[256,1536]{1,0:T(8,128)(2,1)S(1)}, u32[]{:S(2)}, u32[]{:S(2)}) collective-permute-start(bf16[256,1536]{1,0:T(8,128)(2,1)S(1)} %bitcast.76), channel_id=1, source_target_pairs={{0,192},{64,0},{128,64},{192,128},{1,193},{65,1},{129,65},{193,129... | collective-permute-start | bytes 2359304 | tf_op jit(solution)/shard_map/ppermute | solution.py:307
  164.6 17.9 %collective-permute-start.14 = (bf16[256,1536]{1,0:T(8,128)(2,1)S(1)}, bf16[256,1536]{1,0:T(8,128)(2,1)S(1)}, u32[]{:S(2)}, u32[]{:S(2)}) collective-permute-start(bf16[256,1536]{1,0:T(8,128)(2,1)S(1)} %bitcast.75), channel_id=1, source_target_pairs={{0,64},{64,128},{128,192},{192,0},{1,65},{65,129},{129,193},{193,1... | collective-permute-start | bytes 2359304 | tf_op jit(solution)/shard_map/ppermute | solution.py:307
  182.4 24.9 %collective-permute-start.17 = (bf16[256,1536]{1,0:T(8,128)(2,1)}, bf16[256,1536]{1,0:T(8,128)(2,1)S(1)}, u32[]{:S(2)}, u32[]{:S(2)}) collective-permute-start(bf16[256,1536]{1,0:T(8,128)(2,1)} %shard_map.122), channel_id=1, source_target_pairs={{0,64},{64,128},{128,192},{192,0},{1,65},{65,129},{129,193},{193,1... | collective-permute-start | bytes 2359304 | tf_op jit(solution)/shard_map/ppermute | solution.py:307
  190.9 16.5 %collective-permute-start.15 = (bf16[256,1536]{1,0:T(8,128)(2,1)S(1)}, bf16[256,1536]{1,0:T(8,128)(2,1)S(1)}, u32[]{:S(2)}, u32[]{:S(2)}) collective-permute-start(bf16[256,1536]{1,0:T(8,128)(2,1)S(1)} %shard_map.121), channel_id=1, source_target_pairs={{0,192},{64,0},{128,64},{192,128},{1,193},{65,1},{129,65},{193,129... | collective-permute-start | bytes 2359304 | tf_op jit(solution)/shard_map/ppermute | solution.py:307
  211.9 24.5 %copy-start.9 = (bf16[8,128,1536]{2,1,0:T(8,128)(2,1)S(1)}, bf16[8,128,1536]{2,1,0:T(8,128)(2,1)}, u32[]{:S(2)}) copy-start(bf16[8,128,1536]{2,1,0:T(8,128)(2,1)} %get-tuple-element.33) | copy-start | bytes 9437188
  213.3 8.8 %collective-permute-start.18 = (bf16[64,1536]{1,0:T(8,128)(2,1)S(1)}, bf16[64,1536]{1,0:T(8,128)(2,1)S(1)}, u32[]{:S(2)}, u32[]{:S(2)}) collective-permute-start(bf16[64,1536]{1,0:T(8,128)(2,1)S(1)} %get-tuple-element.38), channel_id=1, source_target_pairs={{0,56},{8,0},{16,8},{24,16},{32,24},{40,32},{48,40},{56,48},{1,57}... | collective-permute-start | bytes 589832 | tf_op jit(solution)/shard_map/ppermute | solution.py:307
  216.8 6.9 %collective-permute-start.22 = (bf16[64,1536]{1,0:T(8,128)(2,1)S(1)}, bf16[64,1536]{1,0:T(8,128)(2,1)S(1)}, u32[]{:S(2)}, u32[]{:S(2)}) collective-permute-start(bf16[64,1536]{1,0:T(8,128)(2,1)S(1)} %get-tuple-element.39), channel_id=1, source_target_pairs={{0,8},{8,16},{16,24},{24,32},{32,40},{40,48},{48,56},{56,0},{1,9},... | collective-permute-start | bytes 589832 | tf_op jit(solution)/shard_map/ppermute | solution.py:307
  224.8 11.5 %collective-permute-start.19 = (bf16[128,1536]{1,0:T(8,128)(2,1)S(1)}, bf16[128,1536]{1,0:T(8,128)(2,1)S(1)}, u32[]{:S(2)}, u32[]{:S(2)}) collective-permute-start(bf16[128,1536]{1,0:T(8,128)(2,1)S(1)} %pad_maximum_fusion.1), channel_id=1, source_target_pairs={{0,56},{8,0},{16,8},{24,16},{32,24},{40,32},{48,40},{56,48},{1,57}... | collective-permute-start | bytes 1179656 | tf_op jit(solution)/shard_map/ppermute | solution.py:307
  227.0 13.2 %collective-permute-start.23 = (bf16[128,1536]{1,0:T(8,128)(2,1)S(1)}, bf16[128,1536]{1,0:T(8,128)(2,1)S(1)}, u32[]{:S(2)}, u32[]{:S(2)}) collective-permute-start(bf16[128,1536]{1,0:T(8,128)(2,1)S(1)} %pad_maximum_fusion.2), channel_id=1, source_target_pairs={{0,8},{8,16},{16,24},{24,32},{32,40},{40,48},{48,56},{56,0},{1,9},... | collective-permute-start | bytes 1179656 | tf_op jit(solution)/shard_map/ppermute | solution.py:307
  236.4 9.1 %collective-permute-start.20 = (bf16[128,1536]{1,0:T(8,128)(2,1)S(1)}, bf16[128,1536]{1,0:T(8,128)(2,1)S(1)}, u32[]{:S(2)}, u32[]{:S(2)}) collective-permute-start(bf16[128,1536]{1,0:T(8,128)(2,1)S(1)} %fusion.10), channel_id=1, source_target_pairs={{0,56},{8,0},{16,8},{24,16},{32,24},{40,32},{48,40},{56,48},{1,57}... | collective-permute-start | bytes 1179656 | tf_op jit(solution)/shard_map/ppermute | solution.py:307
  245.7 9.5 %collective-permute-start.24 = (bf16[128,1536]{1,0:T(8,128)(2,1)S(1)}, bf16[128,1536]{1,0:T(8,128)(2,1)S(1)}, u32[]{:S(2)}, u32[]{:S(2)}) collective-permute-start(bf16[128,1536]{1,0:T(8,128)(2,1)S(1)} %get-tuple-element.35), channel_id=1, source_target_pairs={{0,8},{8,16},{16,24},{24,32},{32,40},{40,48},{48,56},{56,0},{1,9},... | collective-permute-start | bytes 1179656 | tf_op jit(solution)/shard_map/ppermute | solution.py:307
  245.8 9.6 %collective-permute-start.21 = (bf16[128,1536]{1,0:T(8,128)(2,1)S(1)}, bf16[128,1536]{1,0:T(8,128)(2,1)S(1)}, u32[]{:S(2)}, u32[]{:S(2)}) collective-permute-start(bf16[128,1536]{1,0:T(8,128)(2,1)S(1)} %get-tuple-element.34), channel_id=1, source_target_pairs={{0,56},{8,0},{16,8},{24,16},{32,24},{40,32},{48,40},{56,48},{1,57}... | collective-permute-start | bytes 1179656 | tf_op jit(solution)/shard_map/ppermute | solution.py:307
  255.3 9.1 %collective-permute-start.25 = (bf16[128,1536]{1,0:T(8,128)(2,1)S(1)}, bf16[128,1536]{1,0:T(8,128)(2,1)S(1)}, u32[]{:S(2)}, u32[]{:S(2)}) collective-permute-start(bf16[128,1536]{1,0:T(8,128)(2,1)S(1)} %fusion.9), channel_id=1, source_target_pairs={{0,8},{8,16},{16,24},{24,32},{32,40},{40,48},{48,56},{56,0},{1,9},... | collective-permute-start | bytes 1179656 | tf_op jit(solution)/shard_map/ppermute | solution.py:307
  (12 other events, 74.5 us)
Sparse Core Ops, SparseCore 0:
  31.5 41.8 all-gather.9
  75.2 37.8 all-gather.5
  114.9 36.8 all-gather.7
